TPU v7x, 32 devices: a whole 2x2x4 slice. The times are simulated.
32 devices in a mesh: groups: 2 (over x), horiz: 16 (over z, y, core).
Axes of the slice: x: 2, y: 2, z: 4, core: 2. Of those that a mesh axis runs over, the one named last changes fastest.
Arguments:
- leaf_nodes: float32 [128, 16, 3072], P('groups', 'horiz'), parts along dimension 0, may hold values from -6 to 6
- compress: float32 [32, 64], replicated, may hold values from -0.75 to 0.75
- expand: float32 [64, 32], replicated, may hold values from -1 to 1
- transfer: float32 [64, 512], replicated, may hold values from -0.25 to 0.25
- m2l_table: float32 [316, 1024], replicated, may hold values from -0.078125 to 0.078125
Outputs:
- leaf_local: float32 [128, 16, 3072], P('groups', 'horiz'), parts along dimension 0
There are 2 independent parts, one for each index of `groups`. A program takes and returns all parts, laid end to end along the dimension named above; an argument that names none is the same for every part. Nothing has to cross between parts.
All inputs are finite; a program needn't handle non-finite values.
Results may differ from a plain program's by a relative error of at most 0.0001.
Values sent between devices are 32-bit elements; how exact they have to be, the bound alone decides.
A program may use at most 128 MiB of HBM per device.

v0:
```python
import functools

import jax
import jax.numpy as jnp
import ml_dtypes
import numpy as np
from jax import lax
from jax.experimental import pallas as pl
from jax.experimental.pallas import tpu as pltpu
from jax.sharding import PartitionSpec as P

GRID_X = 8
PX = 4
PY = 4
PZ = 24
BOXES = PX * PY * PZ
COARSE_Z = 16
COARSE_ROWS = (PX // 2) * (PY // 2) * COARSE_Z
HIGHEST = lax.Precision.HIGHEST
BF16 = jnp.bfloat16
F32 = jnp.float32
DIRECTIONS = [(0, -1), (0, 1), (-1, 0), (1, 0), (-1, -1), (-1, 1), (1, -1), (1, 1)]
RIM_ROWS = PX * PZ + (PX // 2) * COARSE_Z
NT = (((1,), (1,)), ((), ()))


def table_selection():
    select = np.zeros((8 * 56, 316), np.float32)
    row = 0
    for dx in range(7):
        for dy in range(7):
            for dz in range(7):
                if max(abs(dx - 3), abs(dy - 3), abs(dz - 3)) >= 2:
                    select[dz * 56 + dx * 7 + dy, row] = 1.0
                    row += 1
    return select.astype(ml_dtypes.bfloat16)


def parent_selection():
    select = np.zeros((8 * COARSE_ROWS, BOXES), np.float32)
    for bx in range(PX):
        for by in range(PY):
            for bz in range(PZ):
                child = 4 * (bx % 2) + 2 * (by % 2) + bz % 2
                parent = ((bx // 2) * (PY // 2) + by // 2) * COARSE_Z + bz // 2
                select[child * COARSE_ROWS + parent, (bx * PY + by) * PZ + bz] = 1.0
    return select.astype(ml_dtypes.bfloat16)


def split(value):
    high = value.astype(BF16)
    return high, (value - high.astype(F32)).astype(BF16)


def select_dot(value, select, dims):
    high, low = split(value)
    return lax.dot_general(high, select, dims, preferred_element_type=F32) + lax.dot_general(
        low, select, dims, preferred_element_type=F32
    )


def weights_kernel(table_ref, select_ref, high_ref, low_ref, cube, lanes_a, lanes_b):
    table_high, table_low = split(table_ref[...])
    select = select_ref[...]
    cube[...] = jnp.dot(select, table_high, preferred_element_type=F32) + jnp.dot(
        select, table_low, preferred_element_type=F32
    )
    slot = lax.broadcasted_iota(jnp.int32, (56, 128), 1) // 32
    for half, out in enumerate((lanes_a, lanes_b)):
        for tile in range(8):
            parts = [
                cube[(4 * half + k) * 56 : (4 * half + k + 1) * 56, tile * 128 : (tile + 1) * 128]
                for k in range(4)
            ]
            for inner in range(4):
                merged = None
                for k in range(4):
                    by = (k - inner) % 4 * 32
                    moved = pltpu.roll(parts[k], by, 1) if by else parts[k]
                    merged = moved if merged is None else jnp.where(slot == k, moved, merged)
                out[pl.ds(tile * 4 + inner, 56, stride=32), :] = merged
    low_half = lax.broadcasted_iota(jnp.int32, (192, 128), 1) < 64
    lane = lax.broadcasted_iota(jnp.int32, (224, 128), 1)
    for dx in range(7):
        even0 = lanes_a[dx * 224 : (dx + 1) * 224, :]
        even1 = lanes_b[dx * 224 : (dx + 1) * 224, :]
        turned0 = pltpu.roll(even0, 96, 1)
        turned1 = pltpu.roll(even1, 96, 1)
        odd0 = jnp.where(lane < 96, turned0, turned1)
        odd1 = turned1
        for w, (source, straight) in enumerate(
            ((even0, True), (odd0, True), (even0, False), (odd0, False), (even1, True), (odd1, True))
        ):
            other = pltpu.roll(source, 64, 1)
            first, second = (source, other) if straight else (other, source)
            high, low = split(jnp.where(low_half, first[:192], second[32:]))
            high_ref[w * 7 + dx] = high
            low_ref[w * 7 + dx] = low


def charges_kernel(
    grid_rows, leaf_ref, compress_ref, transfer_ref, select_ref, fine_ref, coarse_ref, halo_ref,
    rim, send_sem, recv_sem,
):
    here = lax.axis_index("horiz")
    tile_x = here // grid_rows
    tile_y = here % grid_rows

    def present(dx, dy):
        x, y = tile_x + dx, tile_y + dy
        return (x >= 0) & (x < GRID_X) & (y >= 0) & (y < grid_rows)

    barrier = pltpu.get_barrier_semaphore()
    for dx, dy in DIRECTIONS:
        @pl.when(present(dx, dy))
        def _(dx=dx, dy=dy):
            pl.semaphore_signal(
                barrier, inc=1, device_id={"horiz": here + dx * grid_rows + dy},
                device_id_type=pl.DeviceIdType.MESH,
            )

    compress = compress_ref[...]
    fine, nodes = [], None
    for child in range(8):
        leaf = leaf_ref[:, child * BOXES : (child + 1) * BOXES]
        fine.append(jnp.dot(compress, leaf, precision=HIGHEST, preferred_element_type=F32))
        term = jnp.dot(
            transfer_ref[:, child * 64 : (child + 1) * 64], leaf, precision=HIGHEST,
            preferred_element_type=F32,
        )
        nodes = term if nodes is None else nodes + term
    fine_ref[...] = jnp.concatenate(fine, axis=0).T
    coarse = jnp.dot(compress, nodes, precision=HIGHEST, preferred_element_type=F32)
    grouped = select_dot(coarse, select_ref[...], NT)
    coarse_ref[...] = jnp.concatenate(
        [grouped[:, c * COARSE_ROWS : (c + 1) * COARSE_ROWS] for c in range(8)], axis=0
    ).T

    def pick(step, extent):
        return range(extent) if step == 0 else ([extent - 1] if step > 0 else [0])

    lengths = []
    for number, (dx, dy) in enumerate(DIRECTIONS):
        at = 0
        for x in pick(dx, PX):
            for y in pick(dy, PY):
                start = (x * PY + y) * PZ
                rim[number, at : at + PZ, :] = fine_ref[start : start + PZ, :]
                at += PZ
        for x in pick(dx, PX // 2):
            for y in pick(dy, PY // 2):
                start = (x * (PY // 2) + y) * COARSE_Z
                rim[number, at : at + COARSE_Z, :] = coarse_ref[start : start + COARSE_Z, :]
                at += COARSE_Z
        lengths.append(at)

    peers = sum(jnp.where(present(dx, dy), 1, 0) for dx, dy in DIRECTIONS)
    pl.semaphore_wait(barrier, peers)

    def copy_of(number):
        dx, dy = DIRECTIONS[number]
        return pltpu.make_async_remote_copy(
            src_ref=rim.at[number, pl.ds(0, lengths[number])],
            dst_ref=halo_ref.at[number, pl.ds(0, lengths[number])],
            send_sem=send_sem.at[number],
            recv_sem=recv_sem.at[number],
            device_id={"horiz": here + dx * grid_rows + dy},
            device_id_type=pl.DeviceIdType.MESH,
        )

    for number, (dx, dy) in enumerate(DIRECTIONS):
        @pl.when(present(dx, dy))
        def _(number=number):
            copy_of(number).start()

    for number, (dx, dy) in enumerate(DIRECTIONS):
        @pl.when(jnp.logical_not(present(-dx, -dy)))
        def _(number=number):
            halo_ref[number] = jnp.zeros(halo_ref.shape[1:], F32)

    for number, (dx, dy) in enumerate(DIRECTIONS):
        @pl.when(present(dx, dy))
        def _(number=number):
            copy_of(number).wait_send()

        @pl.when(present(-dx, -dy))
        def _(number=number):
            copy_of(number).wait_recv()


def field_kernel(
    fine_ref, coarse_ref, halo_ref, high_ref, low_ref, expand_ref, transfer_ref, select_ref, out_ref,
    wide, wide_coarse, wins_high, wins_low, cwins_high, cwins_low, total,
):
    zero_rows = jnp.zeros((8, 256), F32)

    def place(x, y, rows):
        wide[x, y, 0:8, :] = zero_rows
        wide[x, y, 8 : 8 + PZ, :] = rows
        wide[x, y, 8 + PZ : 16 + PZ, :] = zero_rows

    def place_coarse(x, y, rows):
        wide_coarse[x, y, 0:8, :] = zero_rows
        wide_coarse[x, y, 8 : 8 + COARSE_Z, :] = rows
        wide_coarse[x, y, 8 + COARSE_Z : 16 + COARSE_Z, :] = zero_rows

    for x in range(PX):
        for y in range(PY):
            start = (x * PY + y) * PZ
            place(x + 1, y + 1, fine_ref[start : start + PZ, :])
    for x in range(PX // 2):
        for y in range(PY // 2):
            start = (x * (PY // 2) + y) * COARSE_Z
            place_coarse(x + 1, y + 1, coarse_ref[start : start + COARSE_Z, :])

    def rim_places(step, extent):
        return range(1, extent + 1) if step == 0 else ([0] if step > 0 else [extent + 1])

    for number, (dx, dy) in enumerate(DIRECTIONS):
        at = 0
        for x in rim_places(dx, PX):
            for y in rim_places(dy, PY):
                place(x, y, halo_ref[number, at : at + PZ, :])
                at += PZ
        for x in rim_places(dx, PX // 2):
            for y in rim_places(dy, PY // 2):
                place_coarse(x, y, halo_ref[number, at : at + COARSE_Z, :])
                at += COARSE_Z

    span = PY * PZ
    for sy in range(3):
        for sz in range(3):
            for x in range(PX + 2):
                rows = jnp.concatenate(
                    [wide[x, sy + y, 7 + sz : 7 + sz + PZ, :] for y in range(PY)], axis=0
                )
                high, low = split(rows)
                wins_high[sy, x * span : (x + 1) * span, sz * 256 : (sz + 1) * 256] = high
                wins_low[sy, x * span : (x + 1) * span, sz * 256 : (sz + 1) * 256] = low
            for sx in range(3):
                rows = jnp.concatenate(
                    [
                        wide_coarse[sx + x, sy + y, 7 + sz : 7 + sz + COARSE_Z, :]
                        for x in range(PX // 2)
                        for y in range(PY // 2)
                    ],
                    axis=0,
                )
                high, low = split(rows)
                cwins_high[sx * 3 + sy, :, sz * 256 : (sz + 1) * 256] = high
                cwins_low[sx * 3 + sy, :, sz * 256 : (sz + 1) * 256] = low

    total[...] = jnp.zeros_like(total)

    def weight(ref, sx, sy, sz):
        rows = []
        for target in range(8):
            tx, ty, tz = target >> 2, target >> 1 & 1, target & 1
            at_y = pl.multiple_of((2 * sy + 1 - ty) * 32, 32)
            first = (2 * sz + 1 - tz) * 7 + 2 * sx + 1 - tx
            rows.append(
                jnp.concatenate(
                    [ref[first, pl.ds(at_y, 32), :], ref[first + 1, pl.ds(at_y, 32), :]], axis=1
                )
            )
        return jnp.concatenate(rows, axis=0)

    def step(at, carry):
        sx, sy = at // 3, at % 3
        rows = pl.ds(pl.multiple_of(sx * span, 32), PX * span)
        high = jnp.concatenate([wins_high[sy, rows, :], cwins_high[at]], axis=0)
        low = jnp.concatenate([wins_low[sy, rows, :], cwins_low[at]], axis=0)
        by_high = jnp.concatenate([weight(high_ref, sx, sy, sz) for sz in range(3)], axis=1)
        by_low = jnp.concatenate([weight(low_ref, sx, sy, sz) for sz in range(3)], axis=1)
        total[...] += lax.dot_general(
            jnp.concatenate([high, low, high], axis=1),
            jnp.concatenate([by_high, by_high, by_low], axis=1),
            NT,
            preferred_element_type=F32,
        )
        return carry

    lax.fori_loop(0, 9, step, 0)

    expand = expand_ref[...]
    local = jnp.concatenate(
        [
            lax.dot_general(
                expand, 0.5 * total[BOXES:, c * 32 : (c + 1) * 32], NT, precision=HIGHEST,
                preferred_element_type=F32,
            )
            for c in range(8)
        ],
        axis=1,
    )
    coarse_local = select_dot(local, select_ref[...], (((1,), (0,)), ((), ())))
    for c in range(8):
        direct = lax.dot_general(
            expand, total[:BOXES, c * 32 : (c + 1) * 32], NT, precision=HIGHEST,
            preferred_element_type=F32,
        )
        pushed = lax.dot_general(
            transfer_ref[:, c * 64 : (c + 1) * 64], coarse_local, (((0,), (0,)), ((), ())),
            precision=HIGHEST, preferred_element_type=F32,
        )
        out_ref[:, c * BOXES : (c + 1) * BOXES] = direct + pushed


LIMIT = 48 * 1024 * 1024
VMEM = pl.BlockSpec(memory_space=pltpu.VMEM)


def shards(leaf_nodes, compress, expand, transfer, m2l_table):
    node_count = leaf_nodes.shape[0]
    grid_rows = lax.axis_size("horiz") // GRID_X
    parents = jnp.asarray(parent_selection())
    fine, coarse, halo = pl.pallas_call(
        functools.partial(charges_kernel, grid_rows),
        out_shape=[
            jax.ShapeDtypeStruct((BOXES, 256), F32),
            jax.ShapeDtypeStruct((COARSE_ROWS, 256), F32),
            jax.ShapeDtypeStruct((8, RIM_ROWS, 256), F32),
        ],
        in_specs=[VMEM] * 4,
        out_specs=[VMEM] * 3,
        scratch_shapes=[
            pltpu.VMEM((8, RIM_ROWS, 256), F32),
            pltpu.SemaphoreType.DMA((8,)),
            pltpu.SemaphoreType.DMA((8,)),
        ],
        compiler_params=pltpu.CompilerParams(
            collective_id=0, has_side_effects=True, vmem_limit_bytes=LIMIT
        ),
        name="charges",
    )(leaf_nodes.reshape(node_count, -1), compress, transfer, parents)
    high, low = pl.pallas_call(
        weights_kernel,
        out_shape=[jax.ShapeDtypeStruct((42, 192, 128), BF16)] * 2,
        in_specs=[VMEM] * 2,
        out_specs=[VMEM] * 2,
        scratch_shapes=[
            pltpu.VMEM((8 * 56, 1024), F32),
            pltpu.VMEM((56 * 32, 128), F32),
            pltpu.VMEM((56 * 32, 128), F32),
        ],
        compiler_params=pltpu.CompilerParams(vmem_limit_bytes=LIMIT),
        name="weights",
    )(m2l_table, jnp.asarray(table_selection()))
    result = pl.pallas_call(
        field_kernel,
        out_shape=jax.ShapeDtypeStruct((node_count, 8 * BOXES), F32),
        in_specs=[VMEM] * 8,
        out_specs=VMEM,
        scratch_shapes=[
            pltpu.VMEM((PX + 2, PY + 2, PZ + 16, 256), F32),
            pltpu.VMEM((PX // 2 + 2, PY // 2 + 2, COARSE_Z + 16, 256), F32),
            pltpu.VMEM((3, (PX + 2) * PY * PZ, 768), BF16),
            pltpu.VMEM((3, (PX + 2) * PY * PZ, 768), BF16),
            pltpu.VMEM((9, COARSE_ROWS, 768), BF16),
            pltpu.VMEM((9, COARSE_ROWS, 768), BF16),
            pltpu.VMEM((BOXES + COARSE_ROWS, 256), F32),
        ],
        compiler_params=pltpu.CompilerParams(vmem_limit_bytes=LIMIT),
        name="field",
    )(fine, coarse, halo, high, low, expand, transfer, parents)
    return result.reshape(node_count, 1, -1)


def solution(mesh):
    return jax.shard_map(
        shards,
        mesh=mesh,
        in_specs=(P("groups", "horiz", None), P(), P(), P(), P()),
        out_specs=P("groups", "horiz", None),
        check_vma=False,
    )
```

profile of v0, /device:TPU:9, one launch (start us, length us, event | category | flops | bytes accessed | tf_op | source)
XLA Modules:
  0.0 36.6 jit_solution(17595468468480139694)
XLA Ops:
  0.0 0.0 copy-start.6
  0.0 0.8 %copy.8.expand_ref = f32[64,32]{1,0:T(8,128)S(1)} copy(f32[64,32]{0,1:T(8,128)} %param.9) | data formatting | bytes 16384 | tf_op args[2]
  0.8 0.0 copy-start.2
  0.9 0.0 copy-start.5
  0.9 1.3 %copy.12 = f32[64,1,3072]{2,0,1:T(8,128)S(1)} copy(f32[64,1,3072]{2,1,0:T(1,128)} %param.7) | data formatting | bytes 1572864
  2.2 0.0 copy-start.1
  2.2 1.0 %copy-done.1 = bf16[512,384]{1,0:T(8,128)(2,1)S(1)} copy-done((bf16[512,384]{1,0:T(8,128)(2,1)S(1)}, bf16[512,384]{1,0:T(8,128)(2,1)}, u32[]{:S(2)}) %copy-start.1) | copy-done | bytes 393240
  3.2 0.0 copy-start.4
  3.2 0.9 %copy-done.4 = f32[64,512]{1,0:T(8,128)S(1)} copy-done((f32[64,512]{1,0:T(8,128)S(1)}, f32[64,512]{1,0:T(8,128)}, u32[]{:S(2)}) %copy-start.4) | copy-done | bytes 131096
  4.1 0.0 copy-start.7
  4.1 0.7 %copy-done.7 = f32[32,64]{1,0:T(8,128)S(1)} copy-done((f32[32,64]{1,0:T(8,128)S(1)}, f32[32,64]{1,0:T(8,128)}, u32[]{:S(2)}) %copy-start.7) | copy-done | bytes 8216
  4.8 0.0 copy-start.3
  4.8 11.6 %charges.1 = (f32[384,256]{1,0:T(8,128)S(1)}, f32[64,256]{1,0:T(8,128)S(1)}, f32[8,128,256]{2,1,0:T(8,128)S(1)}) custom-call(f32[64,3072]{1,0:T(8,128)S(1)} %bitcast.4, f32[32,64]{1,0:T(8,128)S(1)} %copy-done.7, f32[64,512]{1,0:T(8,128)S(1)} %copy-done.4, bf16[512,384]{1,0:T(8,128)(2,1)S(1)} %copy-done.1), custom_call_target="tpu_custom_call" | custom-call | tf_op jit(solution)/shard_map/charges/pallas_call | solution.py:317
  16.5 0.0 copy-done.6
  16.5 0.0 copy-done.3
  16.5 4.1 %weights.1 = (bf16[42,192,128]{2,1,0:T(8,128)(2,1)S(1)}, bf16[42,192,128]{2,1,0:T(8,128)(2,1)S(1)}) custom-call(f32[316,1024]{1,0:T(8,128)S(1)} %copy-done.3, bf16[448,316]{1,0:T(8,128)(2,1)S(1)} %copy-done.6), custom_call_target="tpu_custom_call" | custom-call | tf_op jit(solution)/shard_map/weights/pallas_call | solution.py:336
  20.6 0.0 copy-start
  20.6 1.3 %copy-done = bf16[42,192,128]{2,1,0:T(8,128)(2,1)} copy-done((bf16[42,192,128]{2,1,0:T(8,128)(2,1)}, bf16[42,192,128]{2,1,0:T(8,128)(2,1)S(1)}, u32[]{:S(2)}) %copy-start) | copy-done | bytes 2064408
  22.0 0.0 copy-done.2
  22.0 0.0 copy-done.5
  22.0 12.9 %field.1 = f32[64,3072]{1,0:T(8,128)S(1)} custom-call(f32[384,256]{1,0:T(8,128)S(1)} %get-tuple-element.10.fine_ref, f32[64,256]{1,0:T(8,128)S(1)} %get-tuple-element.11.coarse_ref, f32[8,128,256]{2,1,0:T(8,128)S(1)} %get-tuple-element.12.halo_ref, bf16[42,192,128]{2,1,0:T(8,128)(2,1)S(1)} %get-tuple-element.13.high_ref, bf16[42,192,128]{2,1,0:T(8,128)(2,1)} %copy-done, ...), custom_call_target="tpu_custom_call" | custom-call | tf_op jit(solution)/shard_map/field/pallas_call | solution.py:349
  34.9 1.7 %copy.9 = f32[64,1,3072]{2,1,0:T(1,128)} copy(f32[64,1,3072]{2,0,1:T(8,128)S(1)} %bitcast.5) | data formatting | bytes 1572864 | tf_op jit(solution)/shard_map/reshape | solution.py:366
Async XLA Ops:
  0.0 16.5 %copy-start.6 = (bf16[448,316]{1,0:T(8,128)(2,1)S(1)}, bf16[448,316]{1,0:T(8,128)(2,1)}, u32[]{:S(2)}) copy-start(bf16[448,316]{1,0:T(8,128)(2,1)} %constant.5.clone.select_ref) | copy-start | bytes 849412
  0.8 21.1 %copy-start.2 = (bf16[512,384]{1,0:T(8,128)(2,1)S(1)}, bf16[512,384]{1,0:T(8,128)(2,1)}, u32[]{:S(2)}) copy-start(bf16[512,384]{1,0:T(8,128)(2,1)} %constant.4.clone.select_ref) | copy-start | bytes 1179652
  0.9 21.1 %copy-start.5 = (f32[64,512]{1,0:T(8,128)S(1)}, f32[64,512]{1,0:T(8,128)}, u32[]{:S(2)}) copy-start(f32[64,512]{1,0:T(8,128)} %transfer_ref.3) | copy-start | bytes 393220
  2.2 1.0 %copy-start.1 = (bf16[512,384]{1,0:T(8,128)(2,1)S(1)}, bf16[512,384]{1,0:T(8,128)(2,1)}, u32[]{:S(2)}) copy-start(bf16[512,384]{1,0:T(8,128)(2,1)} %constant.4.clone.select_ref) | copy-start | bytes 1179652
  3.2 0.9 %copy-start.4 = (f32[64,512]{1,0:T(8,128)S(1)}, f32[64,512]{1,0:T(8,128)}, u32[]{:S(2)}) copy-start(f32[64,512]{1,0:T(8,128)} %transfer_ref.3) | copy-start | bytes 393220
  4.1 0.7 %copy-start.7 = (f32[32,64]{1,0:T(8,128)S(1)}, f32[32,64]{1,0:T(8,128)}, u32[]{:S(2)}) copy-start(f32[32,64]{1,0:T(8,128)} %compress_ref.1) | copy-start | bytes 24580
  4.8 11.7 %copy-start.3 = (f32[316,1024]{1,0:T(8,128)S(1)}, f32[316,1024]{1,0:T(8,128)}, u32[]{:S(2)}) copy-start(f32[316,1024]{1,0:T(8,128)} %table_ref.1) | copy-start | bytes 3883012
  20.6 1.3 %copy-start = (bf16[42,192,128]{2,1,0:T(8,128)(2,1)}, bf16[42,192,128]{2,1,0:T(8,128)(2,1)S(1)}, u32[]{:S(2)}) copy-start(bf16[42,192,128]{2,1,0:T(8,128)(2,1)S(1)} %get-tuple-element.14.low_ref) | copy-start | bytes 6193156
where the time goes:
time: 36.9 us; the launch traced here: 36.6 us
  Pallas kernels  28.7 us (78%)
  local copies, waits for them, and re-layouts  7.83 us (21%)
    pallas_call x1, Pallas kernels, shards(): pl.pallas_call(field_kernel, out_shape=jax.ShapeDtypeStruct((node_count,...  12.9 us
    pallas_call x1, Pallas kernels, shards(): pl.pallas_call(functools.partial(charges_kernel, grid_rows), out_shape=[j...  11.6 us
    unnamed x18, local copies, waits for them, and re-layouts  6.14 us
    pallas_call x1, Pallas kernels, shards(): pl.pallas_call(weights_kernel, out_shape=[jax.ShapeDtypeStruct((42, 192,...  4.13 us
    reshape x1, local copies, waits for them, and re-layouts, shards(): return result.reshape(node_count, 1, -1)  1.69 us

commit v1 on v0

--- a/solution.py
+++ b/solution.py
@@ -59,7 +59,7 @@
     )
 
 
-def weights_kernel(table_ref, select_ref, high_ref, low_ref, cube, lanes_a, lanes_b):
+def build_weights(table_ref, select_ref, high_ref, low_ref, cube, lanes_a, lanes_b):
     table_high, table_low = split(table_ref[...])
     select = select_ref[...]
     cube[...] = jnp.dot(select, table_high, preferred_element_type=F32) + jnp.dot(
@@ -99,9 +99,26 @@
 
 
 def charges_kernel(
-    grid_rows, leaf_ref, compress_ref, transfer_ref, select_ref, fine_ref, coarse_ref, halo_ref,
-    rim, send_sem, recv_sem,
+    grid_rows, leaf_hbm, compress_hbm, transfer_hbm, parents_hbm, table_hbm, spread_hbm,
+    fine_ref, coarse_ref, halo_ref, high_ref, low_ref,
+    leaf_ref, compress_ref, transfer_ref, parents_ref, table_ref, spread_ref,
+    cube, lanes_a, lanes_b, rim, load_sem, send_sem, recv_sem,
 ):
+    loads = [
+        pltpu.make_async_copy(source, target, load_sem.at[number])
+        for number, (source, target) in enumerate(
+            (
+                (compress_hbm, compress_ref),
+                (transfer_hbm, transfer_ref),
+                (leaf_hbm.at[:, 0, :], leaf_ref),
+                (parents_hbm, parents_ref),
+                (table_hbm, table_ref),
+                (spread_hbm, spread_ref),
+            )
+        )
+    ]
+    for load in loads:
+        load.start()
     here = lax.axis_index("horiz")
     tile_x = here // grid_rows
     tile_y = here % grid_rows
@@ -119,19 +136,26 @@
                 device_id_type=pl.DeviceIdType.MESH,
             )
 
+    loads[0].wait()
+    loads[1].wait()
     compress = compress_ref[...]
-    fine, nodes = [], None
+    both = jnp.dot(compress, transfer_ref[...], precision=HIGHEST, preferred_element_type=F32)
+    loads[2].wait()
+    fine, coarse = [], None
     for child in range(8):
-        leaf = leaf_ref[:, child * BOXES : (child + 1) * BOXES]
-        fine.append(jnp.dot(compress, leaf, precision=HIGHEST, preferred_element_type=F32))
-        term = jnp.dot(
-            transfer_ref[:, child * 64 : (child + 1) * 64], leaf, precision=HIGHEST,
+        high, low = split(leaf_ref[:, child * BOXES : (child + 1) * BOXES])
+        onto = jnp.concatenate([compress, both[:, child * 64 : (child + 1) * 64]], axis=0)
+        onto_high, onto_low = split(onto)
+        charged = jnp.dot(
+            jnp.concatenate([onto_high, onto_low, onto_high], axis=1),
+            jnp.concatenate([high, high, low], axis=0),
             preferred_element_type=F32,
         )
-        nodes = term if nodes is None else nodes + term
+        fine.append(charged[:32])
+        coarse = charged[32:] if coarse is None else coarse + charged[32:]
     fine_ref[...] = jnp.concatenate(fine, axis=0).T
-    coarse = jnp.dot(compress, nodes, precision=HIGHEST, preferred_element_type=F32)
-    grouped = select_dot(coarse, select_ref[...], NT)
+    loads[3].wait()
+    grouped = select_dot(coarse, parents_ref[...], NT)
     coarse_ref[...] = jnp.concatenate(
         [grouped[:, c * COARSE_ROWS : (c + 1) * COARSE_ROWS] for c in range(8)], axis=0
     ).T
@@ -178,6 +202,10 @@
         def _(number=number):
             halo_ref[number] = jnp.zeros(halo_ref.shape[1:], F32)
 
+    loads[4].wait()
+    loads[5].wait()
+    build_weights(table_ref, spread_ref, high_ref, low_ref, cube, lanes_a, lanes_b)
+
     for number, (dx, dy) in enumerate(DIRECTIONS):
         @pl.when(present(dx, dy))
         def _(number=number):
@@ -189,9 +217,22 @@
 
 
 def field_kernel(
-    fine_ref, coarse_ref, halo_ref, high_ref, low_ref, expand_ref, transfer_ref, select_ref, out_ref,
+    fine_ref, coarse_ref, halo_ref, high_ref, low_ref, expand_hbm, transfer_hbm, parents_hbm, out_hbm,
     wide, wide_coarse, wins_high, wins_low, cwins_high, cwins_low, total,
+    expand_ref, transfer_ref, parents_ref, out_ref, load_sem, store_sem,
 ):
+    loads = [
+        pltpu.make_async_copy(source, target, load_sem.at[number])
+        for number, (source, target) in enumerate(
+            (
+                (expand_hbm, expand_ref),
+                (transfer_hbm, transfer_ref),
+                (parents_hbm, parents_ref),
+            )
+        )
+    ]
+    for load in loads:
+        load.start()
     zero_rows = jnp.zeros((8, 256), F32)
 
     def place(x, y, rows):
@@ -282,49 +323,83 @@
 
     lax.fori_loop(0, 9, step, 0)
 
-    expand = expand_ref[...]
-    local = jnp.concatenate(
-        [
-            lax.dot_general(
-                expand, 0.5 * total[BOXES:, c * 32 : (c + 1) * 32], NT, precision=HIGHEST,
-                preferred_element_type=F32,
+    for load in loads:
+        load.wait()
+    expand = expand_ref[...].T
+    pushes = lax.dot_general(
+        transfer_ref[...], expand, (((0,), (0,)), ((), ())), precision=HIGHEST,
+        preferred_element_type=F32,
+    )
+    expand_high, expand_low = split(jnp.concatenate([expand] * 8, axis=1))
+    push_high, push_low = split(pushes)
+    child_of = lax.broadcasted_iota(jnp.int32, (64, 256), 1) // 32
+    nothing = jnp.zeros((64, 256), BF16)
+    spread_high = jnp.concatenate([jnp.where(child_of == c, expand_high, nothing) for c in range(8)])
+    spread_low = jnp.concatenate([jnp.where(child_of == c, expand_low, nothing) for c in range(8)])
+
+    across = (0.5 * total[BOXES:, :]).T
+    across = jnp.concatenate([across[c * 32 : (c + 1) * 32] for c in range(8)], axis=1)
+    coarse_field = select_dot(across, parents_ref[...], (((1,), (0,)), ((), ())))
+    coarse_high, coarse_low = split(coarse_field)
+    field_high, field_low = split(total[:BOXES, :])
+    local = lax.dot_general(
+        jnp.concatenate([spread_high, spread_low, spread_high], axis=1),
+        jnp.concatenate([field_high, field_high, field_low], axis=1),
+        NT,
+        preferred_element_type=F32,
+    ) + jnp.dot(
+        jnp.concatenate([push_high, push_low, push_high], axis=1),
+        jnp.concatenate([coarse_high, coarse_high, coarse_low], axis=0),
+        preferred_element_type=F32,
+    )
+    stores = []
+    for c in range(8):
+        out_ref[:, c * BOXES : (c + 1) * BOXES] = local[c * 64 : (c + 1) * 64]
+        stores.append(
+            pltpu.make_async_copy(
+                out_ref.at[:, pl.ds(c * BOXES, BOXES)],
+                out_hbm.at[:, 0, pl.ds(c * BOXES, BOXES)],
+                store_sem.at[c],
             )
-            for c in range(8)
-        ],
-        axis=1,
-    )
-    coarse_local = select_dot(local, select_ref[...], (((1,), (0,)), ((), ())))
-    for c in range(8):
-        direct = lax.dot_general(
-            expand, total[:BOXES, c * 32 : (c + 1) * 32], NT, precision=HIGHEST,
-            preferred_element_type=F32,
-        )
-        pushed = lax.dot_general(
-            transfer_ref[:, c * 64 : (c + 1) * 64], coarse_local, (((0,), (0,)), ((), ())),
-            precision=HIGHEST, preferred_element_type=F32,
-        )
-        out_ref[:, c * BOXES : (c + 1) * BOXES] = direct + pushed
-
-
-LIMIT = 48 * 1024 * 1024
+        )
+        stores[c].start()
+    for store in stores:
+        store.wait()
+
+
+LIMIT = 24 * 1024 * 1024
 VMEM = pl.BlockSpec(memory_space=pltpu.VMEM)
+HBM = pl.BlockSpec(memory_space=pltpu.HBM)
 
 
 def shards(leaf_nodes, compress, expand, transfer, m2l_table):
     node_count = leaf_nodes.shape[0]
     grid_rows = lax.axis_size("horiz") // GRID_X
     parents = jnp.asarray(parent_selection())
-    fine, coarse, halo = pl.pallas_call(
+    spread = jnp.asarray(table_selection())
+    fine, coarse, halo, high, low = pl.pallas_call(
         functools.partial(charges_kernel, grid_rows),
         out_shape=[
             jax.ShapeDtypeStruct((BOXES, 256), F32),
             jax.ShapeDtypeStruct((COARSE_ROWS, 256), F32),
             jax.ShapeDtypeStruct((8, RIM_ROWS, 256), F32),
+            jax.ShapeDtypeStruct((42, 192, 128), BF16),
+            jax.ShapeDtypeStruct((42, 192, 128), BF16),
         ],
-        in_specs=[VMEM] * 4,
-        out_specs=[VMEM] * 3,
+        in_specs=[HBM] * 6,
+        out_specs=[VMEM] * 5,
         scratch_shapes=[
+            pltpu.VMEM((node_count, 8 * BOXES), F32),
+            pltpu.VMEM(compress.shape, F32),
+            pltpu.VMEM(transfer.shape, F32),
+            pltpu.VMEM(parents.shape, BF16),
+            pltpu.VMEM(m2l_table.shape, F32),
+            pltpu.VMEM(spread.shape, BF16),
+            pltpu.VMEM((8 * 56, 1024), F32),
+            pltpu.VMEM((56 * 32, 128), F32),
+            pltpu.VMEM((56 * 32, 128), F32),
             pltpu.VMEM((8, RIM_ROWS, 256), F32),
+            pltpu.SemaphoreType.DMA((6,)),
             pltpu.SemaphoreType.DMA((8,)),
             pltpu.SemaphoreType.DMA((8,)),
         ],
@@ -332,25 +407,12 @@
             collective_id=0, has_side_effects=True, vmem_limit_bytes=LIMIT
         ),
         name="charges",
-    )(leaf_nodes.reshape(node_count, -1), compress, transfer, parents)
-    high, low = pl.pallas_call(
-        weights_kernel,
-        out_shape=[jax.ShapeDtypeStruct((42, 192, 128), BF16)] * 2,
-        in_specs=[VMEM] * 2,
-        out_specs=[VMEM] * 2,
-        scratch_shapes=[
-            pltpu.VMEM((8 * 56, 1024), F32),
-            pltpu.VMEM((56 * 32, 128), F32),
-            pltpu.VMEM((56 * 32, 128), F32),
-        ],
-        compiler_params=pltpu.CompilerParams(vmem_limit_bytes=LIMIT),
-        name="weights",
-    )(m2l_table, jnp.asarray(table_selection()))
-    result = pl.pallas_call(
+    )(leaf_nodes, compress, transfer, parents, m2l_table, spread)
+    return pl.pallas_call(
         field_kernel,
-        out_shape=jax.ShapeDtypeStruct((node_count, 8 * BOXES), F32),
-        in_specs=[VMEM] * 8,
-        out_specs=VMEM,
+        out_shape=jax.ShapeDtypeStruct(leaf_nodes.shape, F32),
+        in_specs=[VMEM] * 5 + [HBM] * 3,
+        out_specs=HBM,
         scratch_shapes=[
             pltpu.VMEM((PX + 2, PY + 2, PZ + 16, 256), F32),
             pltpu.VMEM((PX // 2 + 2, PY // 2 + 2, COARSE_Z + 16, 256), F32),
@@ -359,11 +421,16 @@
             pltpu.VMEM((9, COARSE_ROWS, 768), BF16),
             pltpu.VMEM((9, COARSE_ROWS, 768), BF16),
             pltpu.VMEM((BOXES + COARSE_ROWS, 256), F32),
+            pltpu.VMEM(expand.shape[::-1], F32),
+            pltpu.VMEM(transfer.shape, F32),
+            pltpu.VMEM(parents.shape, BF16),
+            pltpu.VMEM((node_count, 8 * BOXES), F32),
+            pltpu.SemaphoreType.DMA((3,)),
+            pltpu.SemaphoreType.DMA((8,)),
         ],
         compiler_params=pltpu.CompilerParams(vmem_limit_bytes=LIMIT),
         name="field",
-    )(fine, coarse, halo, high, low, expand, transfer, parents)
-    return result.reshape(node_count, 1, -1)
+    )(fine, coarse, halo, high, low, expand.T, transfer, parents)
 
 
 def solution(mesh):

time: 36.9 us -> 29.8 us (0.81)
  Pallas kernels: 28.7 us -> 23.4 us
  local copies, waits for them, and re-layouts: 7.83 us -> 6.05 us
    pallas_call x2 -> x1, Pallas kernels: 17 us -> 10.5 us  [shards(): pl.pallas_call(field_kernel, out_shape=jax.ShapeDtypeStruct(leaf_nodes.sh...]
    reshape x1 -> x0, local copies, waits for them, and re-layouts: 1.69 us -> none  [shards(): return result.reshape(node_count, 1, -1)]
    pallas_call x1, Pallas kernels: 11.6 us -> 12.9 us  [shards(): pl.pallas_call(functools.partial(charges_kernel, grid_rows), out_shape=[j...]
where the time goes in v1:
time: 29.8 us; the launch traced here: 29.5 us
  Pallas kernels  23.4 us (79%)
  local copies, waits for them, and re-layouts  6.05 us (20%)
    pallas_call x1, Pallas kernels, shards(): pl.pallas_call(functools.partial(charges_kernel, grid_rows), out_shape=[j...  12.9 us
    pallas_call x1, Pallas kernels, shards(): pl.pallas_call(field_kernel, out_shape=jax.ShapeDtypeStruct(leaf_nodes.sh...  10.5 us
    unnamed x18, local copies, waits for them, and re-layouts  6.05 us

profile of v1, /device:TPU:9, one launch (start us, length us, event | category | flops | bytes accessed | tf_op | source)
XLA Modules:
  0.0 29.5 jit_solution(11301497398644696447)
XLA Ops:
  0.0 0.0 copy-start
  0.0 1.0 %copy-done = bf16[512,384]{1,0:T(8,128)(2,1)S(1)} copy-done((bf16[512,384]{1,0:T(8,128)(2,1)S(1)}, bf16[512,384]{1,0:T(8,128)(2,1)}, u32[]{:S(2)}) %copy-start) | copy-done | bytes 393240
  1.0 0.0 copy-start.2
  1.0 1.3 %copy-done.2 = f32[316,1024]{1,0:T(8,128)S(1)} copy-done((f32[316,1024]{1,0:T(8,128)S(1)}, f32[316,1024]{1,0:T(8,128)}, u32[]{:S(2)}) %copy-start.2) | copy-done | bytes 1294360
  2.3 0.0 copy-start.3
  2.3 1.1 %copy-done.3 = f32[64,1,3072]{2,1,0:T(1,128)S(1)} copy-done((f32[64,1,3072]{2,1,0:T(1,128)S(1)}, f32[64,1,3072]{2,1,0:T(1,128)}, u32[]{:S(2)}) %copy-start.3) | copy-done | bytes 786456
  3.4 0.0 copy-start.4
  3.4 0.9 %copy-done.4 = f32[64,512]{1,0:T(8,128)S(1)} copy-done((f32[64,512]{1,0:T(8,128)S(1)}, f32[64,512]{1,0:T(8,128)}, u32[]{:S(2)}) %copy-start.4) | copy-done | bytes 131096
  4.4 0.0 copy-start.6
  4.4 1.0 %copy-done.6 = bf16[448,316]{1,0:T(8,128)(2,1)S(1)} copy-done((bf16[448,316]{1,0:T(8,128)(2,1)S(1)}, bf16[448,316]{1,0:T(8,128)(2,1)}, u32[]{:S(2)}) %copy-start.6) | copy-done | bytes 283160
  5.3 0.0 copy-start.7
  5.3 0.7 %copy-done.7 = f32[32,64]{1,0:T(8,128)S(1)} copy-done((f32[32,64]{1,0:T(8,128)S(1)}, f32[32,64]{1,0:T(8,128)}, u32[]{:S(2)}) %copy-start.7) | copy-done | bytes 8216
  6.0 0.0 copy-start.1
  6.1 0.0 copy-start.5
  6.1 0.0 copy-start.8
  6.1 12.9 %charges.1 = (f32[384,256]{1,0:T(8,128)S(1)}, f32[64,256]{1,0:T(8,128)S(1)}, f32[8,128,256]{2,1,0:T(8,128)S(1)}, bf16[42,192,128]{2,1,0:T(8,128)(2,1)S(1)}, bf16[42,192,128]{2,1,0:T(8,128)(2,1)S(1)}) custom-call(f32[64,1,3072]{2,1,0:T(1,128)S(1)} %copy-done.3, f32[32,64]{1,0:T(8,128)S(1)} %copy-done.7, f32[64,512]{1,0:T(8,128)S(1)} %copy-done.4, ...), custom_call_target="tpu_custom_call" | custom-call | tf_op jit(solution)/shard_map/charges/pallas_call | solution.py:380
  19.0 0.0 copy-done.1
  19.0 0.0 copy-done.5
  19.0 0.0 copy-done.8
  19.0 10.5 %field.1 = f32[64,1,3072]{2,1,0:T(1,128)} custom-call(f32[384,256]{1,0:T(8,128)S(1)} %get-tuple-element.10.fine_ref, f32[64,256]{1,0:T(8,128)S(1)} %get-tuple-element.11.coarse_ref, f32[8,128,256]{2,1,0:T(8,128)S(1)} %get-tuple-element.12.halo_ref, bf16[42,192,128]{2,1,0:T(8,128)(2,1)S(1)} %get-tuple-element.13.high_ref, ...), custom_call_target="tpu_custom_call" | custom-call | tf_op jit(solution)/shard_map/field/pallas_call | solution.py:411
Async XLA Ops:
  0.0 1.0 %copy-start = (bf16[512,384]{1,0:T(8,128)(2,1)S(1)}, bf16[512,384]{1,0:T(8,128)(2,1)}, u32[]{:S(2)}) copy-start(bf16[512,384]{1,0:T(8,128)(2,1)} %constant.4.clone.parents_hbm) | copy-start | bytes 1179652
  1.0 1.3 %copy-start.2 = (f32[316,1024]{1,0:T(8,128)S(1)}, f32[316,1024]{1,0:T(8,128)}, u32[]{:S(2)}) copy-start(f32[316,1024]{1,0:T(8,128)} %table_hbm.1) | copy-start | bytes 3883012
  2.3 1.1 %copy-start.3 = (f32[64,1,3072]{2,1,0:T(1,128)S(1)}, f32[64,1,3072]{2,1,0:T(1,128)}, u32[]{:S(2)}) copy-start(f32[64,1,3072]{2,1,0:T(1,128)} %leaf_hbm.1) | copy-start | bytes 2359300
  3.4 0.9 %copy-start.4 = (f32[64,512]{1,0:T(8,128)S(1)}, f32[64,512]{1,0:T(8,128)}, u32[]{:S(2)}) copy-start(f32[64,512]{1,0:T(8,128)} %transfer_hbm.3) | copy-start | bytes 393220
  4.4 1.0 %copy-start.6 = (bf16[448,316]{1,0:T(8,128)(2,1)S(1)}, bf16[448,316]{1,0:T(8,128)(2,1)}, u32[]{:S(2)}) copy-start(bf16[448,316]{1,0:T(8,128)(2,1)} %constant.5.clone.spread_hbm) | copy-start | bytes 849412
  5.3 0.7 %copy-start.7 = (f32[32,64]{1,0:T(8,128)S(1)}, f32[32,64]{1,0:T(8,128)}, u32[]{:S(2)}) copy-start(f32[32,64]{1,0:T(8,128)} %compress_hbm.1) | copy-start | bytes 24580
  6.0 12.9 %copy-start.1 = (bf16[512,384]{1,0:T(8,128)(2,1)S(1)}, bf16[512,384]{1,0:T(8,128)(2,1)}, u32[]{:S(2)}) copy-start(bf16[512,384]{1,0:T(8,128)(2,1)} %constant.4.clone.parents_hbm) | copy-start | bytes 1179652
  6.1 12.9 %copy-start.5 = (f32[64,512]{1,0:T(8,128)S(1)}, f32[64,512]{1,0:T(8,128)}, u32[]{:S(2)}) copy-start(f32[64,512]{1,0:T(8,128)} %transfer_hbm.3) | copy-start | bytes 393220
  6.1 12.9 %copy-start.8 = (f32[64,32]{0,1:T(8,128)S(1)}, f32[64,32]{0,1:T(8,128)}, u32[]{:S(2)}) copy-start(f32[64,32]{0,1:T(8,128)} %param.9) | copy-start | bytes 24580

commit v2 on v1

--- a/solution.py
+++ b/solution.py
@@ -98,11 +98,13 @@
             low_ref[w * 7 + dx] = low
 
 
-def charges_kernel(
+def far_kernel(
     grid_rows, leaf_hbm, compress_hbm, transfer_hbm, parents_hbm, table_hbm, spread_hbm,
-    fine_ref, coarse_ref, halo_ref, high_ref, low_ref,
+    expand_hbm, out_hbm, fine_ref, coarse_ref, halo_ref, high_ref, low_ref,
     leaf_ref, compress_ref, transfer_ref, parents_ref, table_ref, spread_ref,
     cube, lanes_a, lanes_b, rim, load_sem, send_sem, recv_sem,
+    wide, wide_coarse, wins_high, wins_low, cwins_high, cwins_low, total,
+    expand_ref, out_ref, store_sem,
 ):
     loads = [
         pltpu.make_async_copy(source, target, load_sem.at[number])
@@ -114,6 +116,7 @@
                 (parents_hbm, parents_ref),
                 (table_hbm, table_ref),
                 (spread_hbm, spread_ref),
+                (expand_hbm, expand_ref),
             )
         )
     ]
@@ -206,33 +209,6 @@
     loads[5].wait()
     build_weights(table_ref, spread_ref, high_ref, low_ref, cube, lanes_a, lanes_b)
 
-    for number, (dx, dy) in enumerate(DIRECTIONS):
-        @pl.when(present(dx, dy))
-        def _(number=number):
-            copy_of(number).wait_send()
-
-        @pl.when(present(-dx, -dy))
-        def _(number=number):
-            copy_of(number).wait_recv()
-
-
-def field_kernel(
-    fine_ref, coarse_ref, halo_ref, high_ref, low_ref, expand_hbm, transfer_hbm, parents_hbm, out_hbm,
-    wide, wide_coarse, wins_high, wins_low, cwins_high, cwins_low, total,
-    expand_ref, transfer_ref, parents_ref, out_ref, load_sem, store_sem,
-):
-    loads = [
-        pltpu.make_async_copy(source, target, load_sem.at[number])
-        for number, (source, target) in enumerate(
-            (
-                (expand_hbm, expand_ref),
-                (transfer_hbm, transfer_ref),
-                (parents_hbm, parents_ref),
-            )
-        )
-    ]
-    for load in loads:
-        load.start()
     zero_rows = jnp.zeros((8, 256), F32)
 
     def place(x, y, rows):
@@ -253,6 +229,15 @@
         for y in range(PY // 2):
             start = (x * (PY // 2) + y) * COARSE_Z
             place_coarse(x + 1, y + 1, coarse_ref[start : start + COARSE_Z, :])
+
+    for number, (dx, dy) in enumerate(DIRECTIONS):
+        @pl.when(present(dx, dy))
+        def _(number=number):
+            copy_of(number).wait_send()
+
+        @pl.when(present(-dx, -dy))
+        def _(number=number):
+            copy_of(number).wait_recv()
 
     def rim_places(step, extent):
         return range(1, extent + 1) if step == 0 else ([0] if step > 0 else [extent + 1])
@@ -323,8 +308,7 @@
 
     lax.fori_loop(0, 9, step, 0)
 
-    for load in loads:
-        load.wait()
+    loads[6].wait()
     expand = expand_ref[...].T
     pushes = lax.dot_general(
         transfer_ref[...], expand, (((0,), (0,)), ((), ())), precision=HIGHEST,
@@ -367,8 +351,7 @@
         store.wait()
 
 
-LIMIT = 24 * 1024 * 1024
-VMEM = pl.BlockSpec(memory_space=pltpu.VMEM)
+LIMIT = 58 * 1024 * 1024
 HBM = pl.BlockSpec(memory_space=pltpu.HBM)
 
 
@@ -377,18 +360,17 @@
     grid_rows = lax.axis_size("horiz") // GRID_X
     parents = jnp.asarray(parent_selection())
     spread = jnp.asarray(table_selection())
-    fine, coarse, halo, high, low = pl.pallas_call(
-        functools.partial(charges_kernel, grid_rows),
-        out_shape=[
-            jax.ShapeDtypeStruct((BOXES, 256), F32),
-            jax.ShapeDtypeStruct((COARSE_ROWS, 256), F32),
-            jax.ShapeDtypeStruct((8, RIM_ROWS, 256), F32),
-            jax.ShapeDtypeStruct((42, 192, 128), BF16),
-            jax.ShapeDtypeStruct((42, 192, 128), BF16),
-        ],
-        in_specs=[HBM] * 6,
-        out_specs=[VMEM] * 5,
+    return pl.pallas_call(
+        functools.partial(far_kernel, grid_rows),
+        out_shape=jax.ShapeDtypeStruct(leaf_nodes.shape, F32),
+        in_specs=[HBM] * 7,
+        out_specs=HBM,
         scratch_shapes=[
+            pltpu.VMEM((BOXES, 256), F32),
+            pltpu.VMEM((COARSE_ROWS, 256), F32),
+            pltpu.VMEM((8, RIM_ROWS, 256), F32),
+            pltpu.VMEM((42, 192, 128), BF16),
+            pltpu.VMEM((42, 192, 128), BF16),
             pltpu.VMEM((node_count, 8 * BOXES), F32),
             pltpu.VMEM(compress.shape, F32),
             pltpu.VMEM(transfer.shape, F32),
@@ -399,21 +381,9 @@
             pltpu.VMEM((56 * 32, 128), F32),
             pltpu.VMEM((56 * 32, 128), F32),
             pltpu.VMEM((8, RIM_ROWS, 256), F32),
-            pltpu.SemaphoreType.DMA((6,)),
+            pltpu.SemaphoreType.DMA((7,)),
             pltpu.SemaphoreType.DMA((8,)),
             pltpu.SemaphoreType.DMA((8,)),
-        ],
-        compiler_params=pltpu.CompilerParams(
-            collective_id=0, has_side_effects=True, vmem_limit_bytes=LIMIT
-        ),
-        name="charges",
-    )(leaf_nodes, compress, transfer, parents, m2l_table, spread)
-    return pl.pallas_call(
-        field_kernel,
-        out_shape=jax.ShapeDtypeStruct(leaf_nodes.shape, F32),
-        in_specs=[VMEM] * 5 + [HBM] * 3,
-        out_specs=HBM,
-        scratch_shapes=[
             pltpu.VMEM((PX + 2, PY + 2, PZ + 16, 256), F32),
             pltpu.VMEM((PX // 2 + 2, PY // 2 + 2, COARSE_Z + 16, 256), F32),
             pltpu.VMEM((3, (PX + 2) * PY * PZ, 768), BF16),
@@ -422,15 +392,14 @@
             pltpu.VMEM((9, COARSE_ROWS, 768), BF16),
             pltpu.VMEM((BOXES + COARSE_ROWS, 256), F32),
             pltpu.VMEM(expand.shape[::-1], F32),
-            pltpu.VMEM(transfer.shape, F32),
-            pltpu.VMEM(parents.shape, BF16),
             pltpu.VMEM((node_count, 8 * BOXES), F32),
-            pltpu.SemaphoreType.DMA((3,)),
             pltpu.SemaphoreType.DMA((8,)),
         ],
-        compiler_params=pltpu.CompilerParams(vmem_limit_bytes=LIMIT),
-        name="field",
-    )(fine, coarse, halo, high, low, expand.T, transfer, parents)
+        compiler_params=pltpu.CompilerParams(
+            collective_id=0, has_side_effects=True, vmem_limit_bytes=LIMIT
+        ),
+        name="far",
+    )(leaf_nodes, compress, transfer, parents, m2l_table, spread, expand.T)
 
 
 def solution(mesh):

time: 29.8 us -> 24.7 us (0.83)
  local copies, waits for them, and re-layouts: 6.05 us -> 2.06 us
  Pallas kernels: 23.4 us -> 22.4 us
    unnamed x18 -> x1, local copies, waits for them, and re-layouts: 6.05 us -> 2.06 us
    pallas_call x2 -> x1, Pallas kernels: 23.4 us -> 22.4 us  [shards(): pl.pallas_call(functools.partial(far_kernel, grid_rows), out_shape=jax.Sh...]
where the time goes in v2:
time: 24.7 us; the launch traced here: 24.4 us
  Pallas kernels  22.4 us (91%)
  local copies, waits for them, and re-layouts  2.06 us (8%)
    pallas_call x1, Pallas kernels, shards(): pl.pallas_call(functools.partial(far_kernel, grid_rows), out_shape=jax.Sh...  22.4 us
    unnamed x1, local copies, waits for them, and re-layouts  2.06 us

profile of v2, /device:TPU:9, one launch (start us, length us, event | category | flops | bytes accessed | tf_op | source)
XLA Modules:
  0.0 24.4 jit_solution(9706237064879519010)
XLA Ops:
  0.0 22.4 %far.1 = f32[64,1,3072]{2,1,0:T(1,128)} custom-call(f32[64,1,3072]{2,1,0:T(1,128)} %leaf_hbm.1, f32[32,64]{1,0:T(8,128)} %compress_hbm.1, f32[64,512]{1,0:T(8,128)} %transfer_hbm.1, bf16[512,384]{1,0:T(8,128)(2,1)} %constant.4.clone.parents_hbm, f32[316,1024]{1,0:T(8,128)} %table_hbm.1, bf16[448,316]{1,0:T(8,128)(2,1)} %constant.5.clone.spread_hbm, ...), custom_call_target="tpu_custom_call" | custom-call | tf_op jit(solution)/shard_map/far/pallas_call | solution.py:363
  22.4 2.1 %copy.9 = f32[64,1,3072]{2,1,0:T(1,128)} copy(f32[64,1,3072]{2,1,0:T(1,128)} %far.1) | data formatting | bytes 1572864

commit v3 on v2

--- a/solution.py
+++ b/solution.py
@@ -103,7 +103,7 @@
     expand_hbm, out_hbm, fine_ref, coarse_ref, halo_ref, high_ref, low_ref,
     leaf_ref, compress_ref, transfer_ref, parents_ref, table_ref, spread_ref,
     cube, lanes_a, lanes_b, rim, load_sem, send_sem, recv_sem,
-    wide, wide_coarse, wins_high, wins_low, cwins_high, cwins_low, total,
+    wide, wide_coarse, wins_high, wins_low, total,
     expand_ref, out_ref, store_sem,
 ):
     loads = [
@@ -230,6 +230,69 @@
             start = (x * (PY // 2) + y) * COARSE_Z
             place_coarse(x + 1, y + 1, coarse_ref[start : start + COARSE_Z, :])
 
+    span = PY * PZ
+
+    def windows(sy, columns):
+        for sz in range(3):
+            lanes = slice(sz * 256, (sz + 1) * 256)
+            for x in columns:
+                rows = jnp.concatenate(
+                    [wide[x, sy + y, 7 + sz : 7 + sz + PZ, :] for y in range(PY)], axis=0
+                )
+                high, low = split(rows)
+                wins_high[sy, x * span : (x + 1) * span, lanes] = high
+                wins_low[sy, x * span : (x + 1) * span, lanes] = low
+
+    def coarse_window(sx, sy, sz):
+        return split(
+            jnp.concatenate(
+                [
+                    wide_coarse[sx + x, sy + y, 7 + sz : 7 + sz + COARSE_Z, :]
+                    for x in range(PX // 2)
+                    for y in range(PY // 2)
+                ],
+                axis=0,
+            )
+        )
+
+    def weight(ref, sx, sy, sz):
+        rows = []
+        for target in range(8):
+            tx, ty, tz = target >> 2, target >> 1 & 1, target & 1
+            at_y = (2 * sy + 1 - ty) * 32
+            first = (2 * sz + 1 - tz) * 7 + 2 * sx + 1 - tx
+            rows.append(
+                jnp.concatenate(
+                    [ref[first, at_y : at_y + 32, :], ref[first + 1, at_y : at_y + 32, :]], axis=1
+                )
+            )
+        return jnp.concatenate(rows, axis=0)
+
+    def apply(sx, sy):
+        depths = (0, 2) if sx == 1 and sy == 1 else (0, 1, 2)
+        rows = slice(sx * span, (sx + PX) * span)
+        high, low, by_high, by_low = [], [], [], []
+        for sz in depths:
+            lanes = slice(sz * 256, (sz + 1) * 256)
+            coarse_high, coarse_low = coarse_window(sx, sy, sz)
+            high.append(jnp.concatenate([wins_high[sy, rows, lanes], coarse_high], axis=0))
+            low.append(jnp.concatenate([wins_low[sy, rows, lanes], coarse_low], axis=0))
+            by_high.append(weight(high_ref, sx, sy, sz))
+            by_low.append(weight(low_ref, sx, sy, sz))
+        product = lax.dot_general(
+            jnp.concatenate(high + low + high, axis=1),
+            jnp.concatenate(by_high + by_high + by_low, axis=1),
+            NT,
+            preferred_element_type=F32,
+        )
+        if sx == 1 and sy == 1:
+            total[...] = product
+        else:
+            total[...] += product
+
+    windows(1, range(1, PX + 1))
+    apply(1, 1)
+
     for number, (dx, dy) in enumerate(DIRECTIONS):
         @pl.when(present(dx, dy))
         def _(number=number):
@@ -253,60 +316,13 @@
                 place_coarse(x, y, halo_ref[number, at : at + COARSE_Z, :])
                 at += COARSE_Z
 
-    span = PY * PZ
-    for sy in range(3):
-        for sz in range(3):
-            for x in range(PX + 2):
-                rows = jnp.concatenate(
-                    [wide[x, sy + y, 7 + sz : 7 + sz + PZ, :] for y in range(PY)], axis=0
-                )
-                high, low = split(rows)
-                wins_high[sy, x * span : (x + 1) * span, sz * 256 : (sz + 1) * 256] = high
-                wins_low[sy, x * span : (x + 1) * span, sz * 256 : (sz + 1) * 256] = low
-            for sx in range(3):
-                rows = jnp.concatenate(
-                    [
-                        wide_coarse[sx + x, sy + y, 7 + sz : 7 + sz + COARSE_Z, :]
-                        for x in range(PX // 2)
-                        for y in range(PY // 2)
-                    ],
-                    axis=0,
-                )
-                high, low = split(rows)
-                cwins_high[sx * 3 + sy, :, sz * 256 : (sz + 1) * 256] = high
-                cwins_low[sx * 3 + sy, :, sz * 256 : (sz + 1) * 256] = low
-
-    total[...] = jnp.zeros_like(total)
-
-    def weight(ref, sx, sy, sz):
-        rows = []
-        for target in range(8):
-            tx, ty, tz = target >> 2, target >> 1 & 1, target & 1
-            at_y = pl.multiple_of((2 * sy + 1 - ty) * 32, 32)
-            first = (2 * sz + 1 - tz) * 7 + 2 * sx + 1 - tx
-            rows.append(
-                jnp.concatenate(
-                    [ref[first, pl.ds(at_y, 32), :], ref[first + 1, pl.ds(at_y, 32), :]], axis=1
-                )
-            )
-        return jnp.concatenate(rows, axis=0)
-
-    def step(at, carry):
-        sx, sy = at // 3, at % 3
-        rows = pl.ds(pl.multiple_of(sx * span, 32), PX * span)
-        high = jnp.concatenate([wins_high[sy, rows, :], cwins_high[at]], axis=0)
-        low = jnp.concatenate([wins_low[sy, rows, :], cwins_low[at]], axis=0)
-        by_high = jnp.concatenate([weight(high_ref, sx, sy, sz) for sz in range(3)], axis=1)
-        by_low = jnp.concatenate([weight(low_ref, sx, sy, sz) for sz in range(3)], axis=1)
-        total[...] += lax.dot_general(
-            jnp.concatenate([high, low, high], axis=1),
-            jnp.concatenate([by_high, by_high, by_low], axis=1),
-            NT,
-            preferred_element_type=F32,
-        )
-        return carry
-
-    lax.fori_loop(0, 9, step, 0)
+    windows(1, (0, PX + 1))
+    apply(0, 1)
+    apply(2, 1)
+    for sy in (0, 2):
+        windows(sy, range(PX + 2))
+        for sx in range(3):
+            apply(sx, sy)
 
     loads[6].wait()
     expand = expand_ref[...].T
@@ -388,8 +404,6 @@
             pltpu.VMEM((PX // 2 + 2, PY // 2 + 2, COARSE_Z + 16, 256), F32),
             pltpu.VMEM((3, (PX + 2) * PY * PZ, 768), BF16),
             pltpu.VMEM((3, (PX + 2) * PY * PZ, 768), BF16),
-            pltpu.VMEM((9, COARSE_ROWS, 768), BF16),
-            pltpu.VMEM((9, COARSE_ROWS, 768), BF16),
             pltpu.VMEM((BOXES + COARSE_ROWS, 256), F32),
             pltpu.VMEM(expand.shape[::-1], F32),
             pltpu.VMEM((node_count, 8 * BOXES), F32),

time: 24.7 us -> 23.8 us (0.964)
  Pallas kernels: 22.4 us -> 21.5 us
    pallas_call x1, Pallas kernels: 22.4 us -> 21.5 us  [shards(): pl.pallas_call(functools.partial(far_kernel, grid_rows), out_shape=jax.Sh...]
where the time goes in v3:
time: 23.8 us; the launch traced here: 23.5 us
  Pallas kernels  21.5 us (90%)
  local copies, waits for them, and re-layouts  2.06 us (9%)
    pallas_call x1, Pallas kernels, shards(): pl.pallas_call(functools.partial(far_kernel, grid_rows), out_shape=jax.Sh...  21.5 us
    unnamed x1, local copies, waits for them, and re-layouts  2.06 us

profile of v3, /device:TPU:9, one launch (start us, length us, event | category | flops | bytes accessed | tf_op | source)
XLA Modules:
  0.0 23.5 jit_solution(16996411984499302208)
XLA Ops:
  0.0 21.5 %far.1 = f32[64,1,3072]{2,1,0:T(1,128)} custom-call(f32[64,1,3072]{2,1,0:T(1,128)} %leaf_hbm.1, f32[32,64]{1,0:T(8,128)} %compress_hbm.1, f32[64,512]{1,0:T(8,128)} %transfer_hbm.1, bf16[512,384]{1,0:T(8,128)(2,1)} %constant.4.clone.parents_hbm, f32[316,1024]{1,0:T(8,128)} %table_hbm.1, bf16[448,316]{1,0:T(8,128)(2,1)} %constant.5.clone.spread_hbm, ...), custom_call_target="tpu_custom_call" | custom-call | tf_op jit(solution)/shard_map/far/pallas_call | solution.py:379
  21.5 2.1 %copy.9 = f32[64,1,3072]{2,1,0:T(1,128)} copy(f32[64,1,3072]{2,1,0:T(1,128)} %far.1) | data formatting | bytes 1572864

commit v4 on v3

--- a/solution.py
+++ b/solution.py
@@ -100,11 +100,11 @@
 
 def far_kernel(
     grid_rows, leaf_hbm, compress_hbm, transfer_hbm, parents_hbm, table_hbm, spread_hbm,
-    expand_hbm, out_hbm, fine_ref, coarse_ref, halo_ref, high_ref, low_ref,
+    total_hbm, fine_ref, coarse_ref, halo_ref, high_ref, low_ref,
     leaf_ref, compress_ref, transfer_ref, parents_ref, table_ref, spread_ref,
     cube, lanes_a, lanes_b, rim, load_sem, send_sem, recv_sem,
     wide, wide_coarse, wins_high, wins_low, total,
-    expand_ref, out_ref, store_sem,
+    store_sem,
 ):
     loads = [
         pltpu.make_async_copy(source, target, load_sem.at[number])
@@ -116,7 +116,6 @@
                 (parents_hbm, parents_ref),
                 (table_hbm, table_ref),
                 (spread_hbm, spread_ref),
-                (expand_hbm, expand_ref),
             )
         )
     ]
@@ -324,7 +323,30 @@
         for sx in range(3):
             apply(sx, sy)
 
-    loads[6].wait()
+    store = pltpu.make_async_copy(total, total_hbm, store_sem.at[0])
+    store.start()
+    store.wait()
+
+
+def expansions_kernel(
+    expand_hbm, transfer_hbm, total_hbm, parents_hbm, out_hbm,
+    expand_ref, transfer_ref, total, parents_ref, out_ref, load_sem, store_sem,
+):
+    loads = [
+        pltpu.make_async_copy(source, target, load_sem.at[number])
+        for number, (source, target) in enumerate(
+            (
+                (expand_hbm, expand_ref),
+                (transfer_hbm, transfer_ref),
+                (total_hbm, total),
+                (parents_hbm, parents_ref),
+            )
+        )
+    ]
+    for load in loads:
+        load.start()
+    for load in loads[:2]:
+        load.wait()
     expand = expand_ref[...].T
     pushes = lax.dot_general(
         transfer_ref[...], expand, (((0,), (0,)), ((), ())), precision=HIGHEST,
@@ -337,6 +359,8 @@
     spread_high = jnp.concatenate([jnp.where(child_of == c, expand_high, nothing) for c in range(8)])
     spread_low = jnp.concatenate([jnp.where(child_of == c, expand_low, nothing) for c in range(8)])
 
+    for load in loads[2:]:
+        load.wait()
     across = (0.5 * total[BOXES:, :]).T
     across = jnp.concatenate([across[c * 32 : (c + 1) * 32] for c in range(8)], axis=1)
     coarse_field = select_dot(across, parents_ref[...], (((1,), (0,)), ((), ())))
@@ -376,10 +400,10 @@
     grid_rows = lax.axis_size("horiz") // GRID_X
     parents = jnp.asarray(parent_selection())
     spread = jnp.asarray(table_selection())
-    return pl.pallas_call(
+    total = pl.pallas_call(
         functools.partial(far_kernel, grid_rows),
-        out_shape=jax.ShapeDtypeStruct(leaf_nodes.shape, F32),
-        in_specs=[HBM] * 7,
+        out_shape=jax.ShapeDtypeStruct((BOXES + COARSE_ROWS, 256), F32),
+        in_specs=[HBM] * 6,
         out_specs=HBM,
         scratch_shapes=[
             pltpu.VMEM((BOXES, 256), F32),
@@ -397,7 +421,7 @@
             pltpu.VMEM((56 * 32, 128), F32),
             pltpu.VMEM((56 * 32, 128), F32),
             pltpu.VMEM((8, RIM_ROWS, 256), F32),
-            pltpu.SemaphoreType.DMA((7,)),
+            pltpu.SemaphoreType.DMA((6,)),
             pltpu.SemaphoreType.DMA((8,)),
             pltpu.SemaphoreType.DMA((8,)),
             pltpu.VMEM((PX + 2, PY + 2, PZ + 16, 256), F32),
@@ -405,15 +429,30 @@
             pltpu.VMEM((3, (PX + 2) * PY * PZ, 768), BF16),
             pltpu.VMEM((3, (PX + 2) * PY * PZ, 768), BF16),
             pltpu.VMEM((BOXES + COARSE_ROWS, 256), F32),
-            pltpu.VMEM(expand.shape[::-1], F32),
-            pltpu.VMEM((node_count, 8 * BOXES), F32),
-            pltpu.SemaphoreType.DMA((8,)),
+            pltpu.SemaphoreType.DMA((1,)),
         ],
         compiler_params=pltpu.CompilerParams(
             collective_id=0, has_side_effects=True, vmem_limit_bytes=LIMIT
         ),
         name="far",
-    )(leaf_nodes, compress, transfer, parents, m2l_table, spread, expand.T)
+    )(leaf_nodes, compress, transfer, parents, m2l_table, spread)
+    return pl.pallas_call(
+        expansions_kernel,
+        out_shape=jax.ShapeDtypeStruct(leaf_nodes.shape, F32),
+        in_specs=[HBM] * 4,
+        out_specs=HBM,
+        scratch_shapes=[
+            pltpu.VMEM(expand.shape[::-1], F32),
+            pltpu.VMEM(transfer.shape, F32),
+            pltpu.VMEM((BOXES + COARSE_ROWS, 256), F32),
+            pltpu.VMEM(parents.shape, BF16),
+            pltpu.VMEM((node_count, 8 * BOXES), F32),
+            pltpu.SemaphoreType.DMA((4,)),
+            pltpu.SemaphoreType.DMA((8,)),
+        ],
+        compiler_params=pltpu.CompilerParams(vmem_limit_bytes=LIMIT),
+        name="expansions",
+    )(expand.T, transfer, total, parents)
 
 
 def solution(mesh):

time: 23.8 us -> 22.7 us (0.954)
  local copies, waits for them, and re-layouts: 2.06 us -> 0 us
  Pallas kernels: 21.5 us -> 22.3 us
    pallas_call x0 -> x1, Pallas kernels: none -> 3.64 us  [shards(): pl.pallas_call(expansions_kernel, out_shape=jax.ShapeDtypeStruct(leaf_nod...]
    pallas_call x1, Pallas kernels: 21.5 us -> 18.7 us  [shards(): pl.pallas_call(functools.partial(far_kernel, grid_rows), out_shape=jax.Sh...]
    unnamed x1 -> x0, local copies, waits for them, and re-layouts: 2.06 us -> none
where the time goes in v4:
time: 22.7 us; the launch traced here: 22.3 us
  Pallas kernels  22.3 us (98%)
    pallas_call x1, Pallas kernels, shards(): pl.pallas_call(functools.partial(far_kernel, grid_rows), out_shape=jax.Sh...  18.7 us
    pallas_call x1, Pallas kernels, shards(): pl.pallas_call(expansions_kernel, out_shape=jax.ShapeDtypeStruct(leaf_nod...  3.64 us

profile of v4, /device:TPU:9, one launch (start us, length us, event | category | flops | bytes accessed | tf_op | source)
XLA Modules:
  0.0 22.3 jit_solution(273467237197147249)
XLA Ops:
  0.0 18.7 %far.1.total_hbm = f32[448,256]{1,0:T(8,128)} custom-call(f32[64,1,3072]{2,1,0:T(1,128)} %leaf_hbm.1, f32[32,64]{1,0:T(8,128)} %compress_hbm.1, f32[64,512]{1,0:T(8,128)} %transfer_hbm.3, bf16[512,384]{1,0:T(8,128)(2,1)} %constant.4.clone.parents_hbm, f32[316,1024]{1,0:T(8,128)} %table_hbm.1, bf16[448,316]{1,0:T(8,128)(2,1)} %constant.5.clone.spread_hbm), custom_call_target="tpu_custom_call" | custom-call | tf_op jit(solution)/shard_map/far/pallas_call | solution.py:403
  18.7 3.6 %expansions.1 = f32[64,1,3072]{2,1,0:T(1,128)} custom-call(f32[32,64]{1,0:T(8,128)} %bitcast.1, f32[64,512]{1,0:T(8,128)} %transfer_hbm.3, f32[448,256]{1,0:T(8,128)} %far.1.total_hbm, bf16[512,384]{1,0:T(8,128)(2,1)} %constant.4.clone.parents_hbm), custom_call_target="tpu_custom_call" | custom-call | tf_op jit(solution)/shard_map/expansions/pallas_call | solution.py:439
